TPU v7x, 256 devices: a whole 4x4x8 slice. The times are simulated.
256 devices in a mesh: blk: 32 (over x_hi, z, core), fold: 8 (over x_lo, y).
Axes of the slice: x: 4 (x_hi: 2, x_lo: 2; x = x_hi * 2 + x_lo), y: 4, z: 8, core: 2. Of those that a mesh axis runs over, the one named last changes fastest.
Arguments:
- picture_vectors: bfloat16 [131072, 1152], P(('blk', 'fold')), may hold values from -0.1796875 to 0.1796875
- caption_vectors: bfloat16 [131072, 1152], P(('blk', 'fold')), may hold values from -0.1796875 to 0.1796875
- logit_multiplier: float32 [], replicated, may hold values from 4 to 16
- logit_shift_term: float32 [], replicated, may hold values from -4 to -1
Outputs:
- image_grad: float32 [131072, 1152], P(('blk', 'fold'))
- text_grad: float32 [131072, 1152], P(('blk', 'fold'))
All inputs are finite; a program needn't handle non-finite values.
Results may differ from a plain program's by a relative error of at most 0.013.
Values may be sent and summed in bfloat16 or wider, within the bound.
A program may use at most 64 MiB of HBM per device.

v0:
```python
import jax
import jax.numpy as jnp
from jax import lax
from jax.sharding import PartitionSpec as P

STEPS = 4


def passed_along(value, axis, steps):
    count = lax.axis_size(axis)
    pairs = [(source, (source + steps) % count) for source in range(count)]
    return lax.ppermute(value, axis, pairs)


def unit_rows(raw):
    wide = raw.astype(jnp.float32)
    scale = 1.0 / jnp.sqrt(jnp.sum(wide * wide, axis=-1, keepdims=True) + 1e-06)
    return (scale, wide * scale)


def back_rows(scale, unit, grad):
    inner = jnp.sum(unit * grad, axis=-1, keepdims=True)
    return scale * (grad - unit * inner)


def weighting_table(
    picture_direction, counterpart_tile, logit_multiplier, logit_shift_term, diagonal_tile_flag
):
    similarity_scores = (
        logit_multiplier
        * lax.dot_general(
            picture_direction,
            counterpart_tile,
            (((1,), (1,)), ((), ())),
            preferred_element_type=jnp.float32,
        )
        + logit_shift_term
    )
    sigmoid_outputs = jax.nn.sigmoid(similarity_scores)
    if diagonal_tile_flag:
        sigmoid_outputs = sigmoid_outputs - jnp.eye(sigmoid_outputs.shape[0], dtype=jnp.float32)
    return (logit_multiplier * sigmoid_outputs).astype(jnp.bfloat16)


def text_term(objective_weight, picture_direction):
    return lax.dot_general(
        objective_weight,
        picture_direction,
        (((0,), (0,)), ((), ())),
        preferred_element_type=jnp.float32,
    )


def shards(picture_vectors, caption_vectors, logit_multiplier, logit_shift_term):
    image_scale, image_unit = unit_rows(picture_vectors)
    text_scale, text_unit = unit_rows(caption_vectors)
    picture_direction = image_unit.astype(jnp.bfloat16)
    text_hat = text_unit.astype(jnp.bfloat16)
    hat_image = jnp.zeros(image_unit.shape, jnp.float32)
    counterpart_tile = text_hat
    carried = jnp.zeros(text_unit.shape, jnp.float32)
    for offset_counter in range(STEPS):
        objective_weight = weighting_table(
            picture_direction,
            counterpart_tile,
            logit_multiplier,
            logit_shift_term,
            offset_counter == 0,
        )
        hat_image = hat_image + jnp.dot(
            objective_weight, counterpart_tile, preferred_element_type=jnp.float32
        )
        carried = carried + text_term(objective_weight, picture_direction)
        if offset_counter + 1 < STEPS:
            counterpart_tile = passed_along(counterpart_tile, ("blk", "fold"), 1)
            carried = passed_along(carried.astype(jnp.bfloat16), ("blk", "fold"), 1).astype(
                carried.dtype
            )
    hat_text = passed_along(carried.astype(jnp.bfloat16), ("blk", "fold"), 1 - STEPS).astype(
        carried.dtype
    )
    image_grad = back_rows(image_scale, image_unit, hat_image)
    text_grad = back_rows(text_scale, text_unit, hat_text)
    return (image_grad, text_grad)


def solution(mesh):
    placed = (P(("blk", "fold"), None), P(("blk", "fold"), None), P(), P())
    return jax.shard_map(
        shards,
        mesh=mesh,
        in_specs=placed,
        out_specs=(P(("blk", "fold"), None), P(("blk", "fold"), None)),
        check_vma=False,
    )
```

profile of v0, /device:TPU:246, one launch (start us, length us, event | category | flops | bytes accessed | tf_op | source)
XLA Modules:
  0.0 191.2 jit_solution(7381800906118206664)
XLA Ops:
  0.6 0.0 copy-start.1
  0.6 1.7 fusion.9
  2.3 0.0 copy-done.1
  2.3 0.0 copy-start
  2.3 0.3 fusion.1
  2.6 1.4 collective-permute-start
  4.0 0.0 copy-done
  4.0 0.3 fusion.8
  5.6 1.1 fusion.37
  6.7 0.9 convolution_convert_fusion
  7.6 1.0 collective-permute-start.3
  8.6 23.1 %collective-permute-done = bf16[512,1152]{1,0:T(8,128)(2,1)} collective-permute-done((bf16[512,1152]{1,0:T(8,128)(2,1)S(1)}, bf16[512,1152]{1,0:T(8,128)(2,1)}, u32[]{:S(2)}, u32[]{:S(2)}) %collective-permute-start) | collective-permute-done | bytes 1179680 | tf_op jit(solution)/shard_map/ppermute | solution.py:12
  31.6 24.0 %collective-permute-start.1 = (bf16[512,1152]{1,0:T(8,128)(2,1)}, bf16[512,1152]{1,0:T(8,128)(2,1)S(1)}, u32[]{:S(2)}, u32[]{:S(2)}) collective-permute-start(bf16[512,1152]{1,0:T(8,128)(2,1)} %collective-permute-done), channel_id=1, source_target_pairs={{0,1},{1,2},{2,3},{3,4},{4,5},{5,6},{6,7},{7,8},{8,9},{9,10},{10,1... | collective-permute-start | bytes 3538952 | tf_op jit(solution)/shard_map/ppermute | solution.py:12
  55.6 2.3 %fusion.40 = bf16[512,512]{1,0:T(8,128)(2,1)S(1)} fusion(bf16[512,1152]{1,0:T(8,128)(2,1)} %collective-permute-done, f32[]{:T(128)S(6)} %copy.7, f32[]{:T(128)S(6)} %copy.6, bf16[512,1152]{1,0:T(8,128)(2,1)S(1)} %copy-done, f32[512]{0:T(512)S(1)} %add_rsqrt_fusion.1), kind=kOutput, calls=%fused_computation.57 | convolution fusion | flops 607584256 | bytes 2885640 | tf_op jit(solution)/shard_map/dot_general | solution.py:31
  58.0 0.0 collective-permute-done.3
  58.0 1.0 add_convert_fusion.2
  59.0 23.0 %collective-permute-start.4 = (bf16[512,1152]{1,0:T(8,128)(2,1)S(1)}, bf16[512,1152]{1,0:T(8,128)(2,1)S(1)}, u32[]{:S(2)}, u32[]{:S(2)}) collective-permute-start(bf16[512,1152]{1,0:T(8,128)(2,1)S(1)} %add_convert_fusion.2), channel_id=1, source_target_pairs={{0,1},{1,2},{2,3},{3,4},{4,5},{5,6},{6,7},{7,8},{8,9},{9,10},{10,1... | collective-permute-start | bytes 3538952 | tf_op jit(solution)/shard_map/ppermute | solution.py:12
  82.0 0.4 collective-permute-done.1
  82.4 36.6 %collective-permute-start.2 = (bf16[512,1152]{1,0:T(8,128)(2,1)S(1)}, bf16[512,1152]{1,0:T(8,128)(2,1)S(1)}, u32[]{:S(2)}, u32[]{:S(2)}) collective-permute-start(bf16[512,1152]{1,0:T(8,128)(2,1)S(1)} %collective-permute-done.1), channel_id=1, source_target_pairs={{0,1},{1,2},{2,3},{3,4},{4,5},{5,6},{6,7},{7,8},{8,9},{9,10},{10,1... | collective-permute-start | bytes 3538952 | tf_op jit(solution)/shard_map/ppermute | solution.py:12
  119.0 1.1 fusion.39
  120.0 0.9 fusion.43
  121.0 0.0 collective-permute-done.4
  121.0 0.2 add_convert_fusion.1
  121.2 10.7 %collective-permute-start.5 = (bf16[512,1152]{1,0:T(8,128)(2,1)S(1)}, bf16[512,1152]{1,0:T(8,128)(2,1)S(1)}, u32[]{:S(2)}, u32[]{:S(2)}) collective-permute-start(bf16[512,1152]{1,0:T(8,128)(2,1)S(1)} %add_convert_fusion.1), channel_id=1, source_target_pairs={{0,1},{1,2},{2,3},{3,4},{4,5},{5,6},{6,7},{7,8},{8,9},{9,10},{10,1... | collective-permute-start | bytes 3538952 | tf_op jit(solution)/shard_map/ppermute | solution.py:12
  131.9 0.8 fusion.54
  132.8 2.1 %convolution_add_fusion.2 = f32[512,1152]{1,0:T(8,128)S(1)} fusion(f32[512,1152]{1,0:T(8,128)S(1)} %fusion.54, bf16[512,512]{1,0:T(8,128)(2,1)S(1)} %fusion.40, bf16[512,1152]{1,0:T(8,128)(2,1)} %collective-permute-done), kind=kOutput, calls=%fused_computation.2 | convolution fusion | flops 604569600 | bytes 6422528 | tf_op jit(solution)/shard_map/dot_general | solution.py:70
  134.9 8.0 %collective-permute-done.2 = bf16[512,1152]{1,0:T(8,128)(2,1)S(1)} collective-permute-done((bf16[512,1152]{1,0:T(8,128)(2,1)S(1)}, bf16[512,1152]{1,0:T(8,128)(2,1)S(1)}, u32[]{:S(2)}, u32[]{:S(2)}) %collective-permute-start.2) | collective-permute-done | bytes 1179680 | tf_op jit(solution)/shard_map/ppermute | solution.py:12
  143.0 1.1 fusion.38
  144.0 0.9 fusion.41
  145.0 23.3 %collective-permute-done.5 = bf16[512,1152]{1,0:T(8,128)(2,1)S(1)} collective-permute-done((bf16[512,1152]{1,0:T(8,128)(2,1)S(1)}, bf16[512,1152]{1,0:T(8,128)(2,1)S(1)}, u32[]{:S(2)}, u32[]{:S(2)}) %collective-permute-start.5) | collective-permute-done | bytes 1179680 | tf_op jit(solution)/shard_map/ppermute | solution.py:12
  168.3 0.2 add_convert_fusion
  168.5 0.1 collective-permute-start.6
  168.6 0.8 convolution_add_fusion.1
  169.4 1.1 fusion.5
  170.5 1.9 fusion.7
  172.4 16.3 %collective-permute-done.6 = bf16[512,1152]{1,0:T(8,128)(2,1)S(1)} collective-permute-done((bf16[512,1152]{1,0:T(8,128)(2,1)S(1)}, bf16[512,1152]{1,0:T(8,128)(2,1)S(1)}, u32[]{:S(2)}, u32[]{:S(2)}) %collective-permute-start.6) | collective-permute-done | bytes 1179680 | tf_op jit(solution)/shard_map/ppermute | solution.py:12
  188.7 0.5 fusion.10
  189.3 2.0 %fusion.11 = f32[512,1152]{1,0:T(8,128)} fusion(bf16[512,1152]{1,0:T(8,128)(2,1)S(1)} %copy-done.1, bf16[512,1152]{1,0:T(8,128)(2,1)S(1)} %collective-permute-done.6, f32[512]{0:T(512)S(1)} %fusion.10, f32[512]{0:T(512)S(1)} %add_rsqrt_fusion), kind=kLoop, calls=%fused_computation.21 | loop fusion | flops 3538944 | bytes 4722688 | tf_op jit(solution)/shard_map/mul | solution.py:23
  (2 shorter events, 0.0 us)
Async XLA Ops:
  0.6 1.7 copy-start.1
  2.3 1.6 copy-start
  2.6 29.0 %collective-permute-start = (bf16[512,1152]{1,0:T(8,128)(2,1)S(1)}, bf16[512,1152]{1,0:T(8,128)(2,1)}, u32[]{:S(2)}, u32[]{:S(2)}) collective-permute-start(bf16[512,1152]{1,0:T(8,128)(2,1)S(1)} %fusion.1), channel_id=1, source_target_pairs={{0,1},{1,2},{2,3},{3,4},{4,5},{5,6},{6,7},{7,8},{8,9},{9,10},{10,1... | collective-permute-start | bytes 3538952 | tf_op jit(solution)/shard_map/ppermute | solution.py:12
  7.6 50.4 %collective-permute-start.3 = (bf16[512,1152]{1,0:T(8,128)(2,1)S(1)}, bf16[512,1152]{1,0:T(8,128)(2,1)S(1)}, u32[]{:S(2)}, u32[]{:S(2)}) collective-permute-start(bf16[512,1152]{1,0:T(8,128)(2,1)S(1)} %convolution_convert_fusion), channel_id=1, source_target_pairs={{0,1},{1,2},{2,3},{3,4},{4,5},{5,6},{6,7},{7,8},{8,9},{9,10},{10,1... | collective-permute-start | bytes 3538952 | tf_op jit(solution)/shard_map/ppermute | solution.py:12
  31.6 50.7 %collective-permute-start.1 = (bf16[512,1152]{1,0:T(8,128)(2,1)}, bf16[512,1152]{1,0:T(8,128)(2,1)S(1)}, u32[]{:S(2)}, u32[]{:S(2)}) collective-permute-start(bf16[512,1152]{1,0:T(8,128)(2,1)} %collective-permute-done), channel_id=1, source_target_pairs={{0,1},{1,2},{2,3},{3,4},{4,5},{5,6},{6,7},{7,8},{8,9},{9,10},{10,1... | collective-permute-start | bytes 3538952 | tf_op jit(solution)/shard_map/ppermute | solution.py:12
  59.0 62.0 %collective-permute-start.4 = (bf16[512,1152]{1,0:T(8,128)(2,1)S(1)}, bf16[512,1152]{1,0:T(8,128)(2,1)S(1)}, u32[]{:S(2)}, u32[]{:S(2)}) collective-permute-start(bf16[512,1152]{1,0:T(8,128)(2,1)S(1)} %add_convert_fusion.2), channel_id=1, source_target_pairs={{0,1},{1,2},{2,3},{3,4},{4,5},{5,6},{6,7},{7,8},{8,9},{9,10},{10,1... | collective-permute-start | bytes 3538952 | tf_op jit(solution)/shard_map/ppermute | solution.py:12
  82.4 60.6 %collective-permute-start.2 = (bf16[512,1152]{1,0:T(8,128)(2,1)S(1)}, bf16[512,1152]{1,0:T(8,128)(2,1)S(1)}, u32[]{:S(2)}, u32[]{:S(2)}) collective-permute-start(bf16[512,1152]{1,0:T(8,128)(2,1)S(1)} %collective-permute-done.1), channel_id=1, source_target_pairs={{0,1},{1,2},{2,3},{3,4},{4,5},{5,6},{6,7},{7,8},{8,9},{9,10},{10,1... | collective-permute-start | bytes 3538952 | tf_op jit(solution)/shard_map/ppermute | solution.py:12
  121.2 47.1 %collective-permute-start.5 = (bf16[512,1152]{1,0:T(8,128)(2,1)S(1)}, bf16[512,1152]{1,0:T(8,128)(2,1)S(1)}, u32[]{:S(2)}, u32[]{:S(2)}) collective-permute-start(bf16[512,1152]{1,0:T(8,128)(2,1)S(1)} %add_convert_fusion.1), channel_id=1, source_target_pairs={{0,1},{1,2},{2,3},{3,4},{4,5},{5,6},{6,7},{7,8},{8,9},{9,10},{10,1... | collective-permute-start | bytes 3538952 | tf_op jit(solution)/shard_map/ppermute | solution.py:12
  168.5 20.2 %collective-permute-start.6 = (bf16[512,1152]{1,0:T(8,128)(2,1)S(1)}, bf16[512,1152]{1,0:T(8,128)(2,1)S(1)}, u32[]{:S(2)}, u32[]{:S(2)}) collective-permute-start(bf16[512,1152]{1,0:T(8,128)(2,1)S(1)} %add_convert_fusion), channel_id=1, source_target_pairs={{0,253},{1,254},{2,255},{3,0},{4,1},{5,2},{6,3},{7,4},{8,5},{9,6},... | collective-permute-start | bytes 3538952 | tf_op jit(solution)/shard_map/ppermute | solution.py:12
where the time goes:
time: 191 us
  starting transfers between devices  96.8 us (51%)
  waiting for transfers between devices  71.1 us (37%)
  matrix products  14.2 us (7%)
  other arithmetic  7.06 us (4%)
  between operations  2.07 us (1%)
    ppermute x7, starting transfers between devices, passed_along(): return lax.ppermute(value, axis, pairs)  96.8 us
    ppermute x7, waiting for transfers between devices, passed_along(): return lax.ppermute(value, axis, pairs)  71.1 us
    dot_general x4, matrix products, weighting_table(): lax.dot_general(picture_direction, counterpart_tile, (((1,), (1,)), ((),...  5.5 us
    dot_general x4, matrix products, shards(): jnp.dot(objective_weight, counterpart_tile, preferred_element_type=jnp.fl...  4.93 us
    mul x2, other arithmetic, back_rows(): return scale * (grad - unit * inner)  3.84 us
  transfers between devices with their start and end apart: 7, of which 5 were waited for; matrix products, arithmetic and copies ran while one was open for 9% of the time, Pallas kernels for 0%

commit v1 on v0

v1 whole, which is shorter than its diff:
```python
import functools

import jax
import jax.numpy as jnp
from jax import lax
from jax.experimental import pallas as pl
from jax.experimental.pallas import tpu as pltpu
from jax.sharding import PartitionSpec as P

MESH = pl.DeviceIdType.MESH
PIECES = 8
PARTS = 4
OWN, PARTNER = 0, 1
A, M, X = 0, 1, 2


def kernel(
    total, fold_size, image_ref, text_ref, mult_ref, shift_ref, image_out, text_out,
    raw, imgs, texts, scales, gi, gt, gp_out, gm_out, gx_out, gp_in, gm_in, gx_in, stage,
    load_sem, store_sem, i_send, i_recv, m_send, m_recv, x_send, x_recv,
    gp_send, gp_recv, gm_send, gm_recv, gx_send, gx_recv,
):
    rows, width = raw.shape[1:]
    piece, part = rows // PIECES, rows // PARTS
    per = PIECES // PARTS
    d = lax.axis_index("blk") * fold_size + lax.axis_index("fold")
    y = lax.rem(d, 4)
    odd = lax.rem(y, 2)
    mult, shift = mult_ref[0, 0], shift_ref[0, 0]

    def device(number):
        number = lax.rem(number + total, total)
        return (number // fold_size, lax.rem(number, fold_size))

    def where(*values):
        picked = jnp.int32(values[0])
        for place in range(1, 4):
            picked = jnp.where(y == place, jnp.int32(values[place]), picked)
        return picked

    def among(*places):
        met = y == places[0]
        for place in places[1:]:
            met = jnp.logical_or(met, y == place)
        return met

    def span(f, size=None):
        size = piece if size is None else size
        return pl.ds(pl.multiple_of(f * size, size), size)

    partner = device(d + 1 - 2 * odd)
    m_target = device(d + where(3, 1, 3, -3))
    gm_target = device(d + where(3, 1, -1, -3))

    def remote(src, dst, send, recv, f, target):
        return pltpu.make_async_remote_copy(
            src_ref=src, dst_ref=dst, send_sem=send.at[f], recv_sem=recv.at[f],
            device_id=target, device_id_type=MESH,
        )

    def i_copy(f):
        return remote(imgs.at[OWN, span(f)], imgs.at[PARTNER, span(f)], i_send, i_recv, f, partner)

    def m_copy(f, slot):
        return remote(texts.at[slot, span(f)], texts.at[M, span(f)], m_send, m_recv, f, m_target)

    def x_copy(f):
        return remote(texts.at[A, span(f)], texts.at[X, span(f)], x_send, x_recv, f, device(d + 4))

    def gp_copy(f):
        return remote(gp_out.at[span(f)], gp_in.at[span(f)], gp_send, gp_recv, f, partner)

    def gm_copy(f):
        return remote(gm_out.at[span(f)], gm_in.at[span(f)], gm_send, gm_recv, f, gm_target)

    def gx_copy(f, source):
        return remote(source.at[span(f)], gx_in.at[span(f)], gx_send, gx_recv, f, device(d - 4))

    def load(which, f):
        source = (image_ref, text_ref)[which]
        return pltpu.make_async_copy(
            source.at[span(f)], raw.at[which, span(f)], load_sem.at[which, f]
        )

    barrier = pltpu.get_barrier_semaphore()
    near = {0: (1, 3), 1: (-1, 1, 4, -4, -3), 2: (1, 3, -1, 4, -4), 3: (-1, -3, 4, -4)}
    for f in range(PIECES):
        load(0, f).start()
        load(1, f).start()
    for place, offsets in near.items():

        @pl.when(y == place)
        def _():
            for offset in offsets:
                pl.semaphore_signal(
                    barrier, inc=1, device_id=device(d + offset), device_id_type=MESH
                )

    def normalize(which, f):
        load(which, f).wait()
        wide = raw[which, span(f), :].astype(jnp.float32)
        scale = 1.0 / jnp.sqrt(jnp.sum(wide * wide, axis=-1, keepdims=True) + 1e-06)
        scales[which, span(f), :] = jnp.broadcast_to(scale, (piece, scales.shape[-1]))
        (imgs, texts)[which][0, span(f), :] = (wide * scale).astype(jnp.bfloat16)

    normalize(0, 0)
    normalize(1, 0)
    for place, offsets in near.items():

        @pl.when(y == place)
        def _():
            pl.semaphore_wait(barrier, len(offsets))

    def send_in(f):
        i_copy(f).start()

        @pl.when(y < 3)
        def _():
            m_copy(f, A).start()

        @pl.when(odd == 1)
        def _():
            x_copy(f).start()

    send_in(0)

    @pl.loop(1, PIECES)
    def _(f):
        normalize(0, f)
        normalize(1, f)
        send_in(f)

    def forward(f):
        @pl.when(y == 3)
        def _():
            x_copy(f).wait_recv()
            m_copy(f, X).start()

    def tile(image, i0, i_rows, text, t0, t_rows, diagonal=False, fresh=False):
        pictures = imgs[image, pl.ds(i0, i_rows), :]
        captions = texts[text, pl.ds(t0, t_rows), :]
        scores = lax.dot_general(
            pictures, captions, (((1,), (1,)), ((), ())), preferred_element_type=jnp.float32
        )
        weights = jax.nn.sigmoid(mult * scores + shift)
        if diagonal:
            r = lax.broadcasted_iota(jnp.int32, weights.shape, 0) + i0
            c = lax.broadcasted_iota(jnp.int32, weights.shape, 1) + t0
            weights = jnp.where(r == c, weights - 1.0, weights)
        coeff = (mult * weights).astype(jnp.bfloat16)
        to_image = jnp.dot(coeff, captions, preferred_element_type=jnp.float32)
        to_text = lax.dot_general(
            coeff, pictures, (((0,), (0,)), ((), ())), preferred_element_type=jnp.float32
        )
        if fresh:
            gi[image, pl.ds(i0, i_rows), :] = to_image
        else:
            gi[image, pl.ds(i0, i_rows), :] += to_image
        gt[text, pl.ds(t0, t_rows), :] += to_text

    def at(c):
        return pl.multiple_of(c * part, part)

    forward(0)
    gt[...] = jnp.zeros_like(gt)
    gi[PARTNER] = jnp.zeros_like(gi[PARTNER])

    @pl.loop(0, PARTS)
    def _(c):
        tile(OWN, at(c), part, A, 0, rows, diagonal=True, fresh=True)

    def corner(text, c):
        @pl.loop(0, c)
        def _(k):
            tile(PARTNER, at(k), part, text, at(c), part)

        @pl.loop(0, c + 1)
        def _(k):
            tile(PARTNER, at(c), part, text, at(k), part)

    def arrived(f, with_x):
        i_copy(f).wait_recv()
        m_copy(f, A).wait_recv()
        if with_x:

            @pl.when(y == 1)
            def _():
                x_copy(f).wait_recv()

    def own_with_m(c):
        tile(OWN, 0, rows, M, at(c), part)

    for c in range(PARTS - 1):
        for f in range(c * per, (c + 1) * per):
            if f > 0:
                forward(f)
        for f in range(c * per, (c + 1) * per):
            arrived(f, True)
        own_with_m(c)
        corner(M, c)

        @pl.when(odd == 0)
        def _():
            tile(PARTNER, at(c), part, A, 0, rows)

        @pl.when(odd == 1)
        def _():
            corner(X, c)

    last = PARTS - 1
    for f in range(last * per, PIECES):
        forward(f)
    for f in range(last * per, PIECES):
        arrived(f, True)

    def send_back(grad, out, copy, c):
        out[span(c, part), :] = grad[span(c, part), :].astype(jnp.bfloat16)
        for f in range(per):
            copy(c * per + f).start()

    def give_gp(c):
        send_back(gi.at[PARTNER], gp_out, gp_copy, c)

    def give_gm(c):
        send_back(gt.at[M], gm_out, gm_copy, c)

    def give_gx(c):
        @pl.when(y == 1)
        def _():
            send_back(gt.at[X], gx_out, lambda f: gx_copy(f, gx_out), c)

    @pl.loop(0, last)
    def _(k):
        tile(PARTNER, at(k), part, M, at(last), part)

        @pl.when(odd == 1)
        def _():
            tile(PARTNER, at(k), part, X, at(last), part)

        give_gp(k)
        tile(PARTNER, at(last), part, M, at(k), part)
        give_gm(k)

        @pl.when(odd == 1)
        def _():
            tile(PARTNER, at(last), part, X, at(k), part)

        give_gx(k)

    tile(PARTNER, at(last), part, M, at(last), part)

    @pl.when(odd == 0)
    def _():
        tile(PARTNER, at(last), part, A, 0, rows)

    @pl.when(odd == 1)
    def _():
        tile(PARTNER, at(last), part, X, at(last), part)

    give_gp(last)
    give_gx(last)
    own_with_m(last)
    give_gm(last)

    def store(which, f):
        target = (image_out, text_out)[which]
        slot = lax.rem(f, 2)
        return pltpu.make_async_copy(
            stage.at[which, slot], target.at[span(f)], store_sem.at[which, slot]
        )

    def finish(which, f, grad):
        scale = scales[which, span(f), :][:, :1]
        unit = raw[which, span(f), :].astype(jnp.float32) * scale
        inner = jnp.sum(unit * grad, axis=-1, keepdims=True)

        @pl.when(f >= 2)
        def _():
            store(which, f - 2).wait()

        stage[which, lax.rem(f, 2)] = scale * (grad - unit * inner)
        store(which, f).start()

    def wide(ref, f):
        return ref[span(f), :].astype(jnp.float32)

    def relay(f):
        @pl.when(y == 2)
        def _():
            gm_copy(f).wait_recv()
            gx_copy(f, gm_in).start()

        @pl.when(y == 3)
        def _():
            gm_copy(f).wait_recv()
            gx_out[span(f), :] = (gt[X, span(f), :] + wide(gm_in, f)).astype(jnp.bfloat16)
            gx_copy(f, gx_out).start()

    def finish_image(f):
        gp_copy(f).wait_recv()
        finish(0, f, gi[OWN, span(f), :] + wide(gp_in, f))

    def finish_text(f):
        @pl.when(y < 2)
        def _():
            gm_copy(f).wait_recv()
            gt[A, span(f), :] += wide(gm_in, f)

        @pl.when(y > 0)
        def _():
            gx_copy(f, gx_out).wait_recv()
            gt[A, span(f), :] += wide(gx_in, f)

        finish(1, f, gt[A, span(f), :])

    @pl.loop(0, PIECES)
    def _(f):
        relay(f)
        finish_image(f)

        @pl.when(f >= 1)
        def _():
            finish_text(f - 1)

    finish_text(PIECES - 1)

    @pl.loop(0, PIECES)
    def _(f):
        i_copy(f).wait_send()
        m_copy(f, A).wait_send()
        gp_copy(f).wait_send()
        gm_copy(f).wait_send()

        @pl.when(odd == 1)
        def _():
            x_copy(f).wait_send()

        @pl.when(y > 0)
        def _():
            gx_copy(f, gx_out).wait_send()

    for f in range(PIECES - 2, PIECES):
        store(0, f).wait()
        store(1, f).wait()


def solution(mesh):
    fold_size = mesh.shape["fold"]
    total = fold_size * mesh.shape["blk"]

    def shards(picture_vectors, caption_vectors, logit_multiplier, logit_shift_term):
        rows, width = picture_vectors.shape
        block = (rows, width)
        dma = pltpu.SemaphoreType.DMA
        return pl.pallas_call(
            functools.partial(kernel, total, fold_size),
            out_shape=(jax.ShapeDtypeStruct(block, jnp.float32),) * 2,
            in_specs=[pl.BlockSpec(memory_space=pl.ANY)] * 2
            + [pl.BlockSpec(memory_space=pltpu.SMEM)] * 2,
            out_specs=(pl.BlockSpec(memory_space=pl.ANY),) * 2,
            scratch_shapes=[
                pltpu.VMEM((2,) + block, jnp.bfloat16),
                pltpu.VMEM((2,) + block, jnp.bfloat16),
                pltpu.VMEM((3,) + block, jnp.bfloat16),
                pltpu.VMEM((2, rows, 128), jnp.float32),
                pltpu.VMEM((2,) + block, jnp.float32),
                pltpu.VMEM((3,) + block, jnp.float32),
                pltpu.VMEM(block, jnp.bfloat16),
                pltpu.VMEM(block, jnp.bfloat16),
                pltpu.VMEM(block, jnp.bfloat16),
                pltpu.VMEM(block, jnp.bfloat16),
                pltpu.VMEM(block, jnp.bfloat16),
                pltpu.VMEM(block, jnp.bfloat16),
                pltpu.VMEM((2, 2, rows // PIECES, width), jnp.float32),
                dma((2, PIECES)),
                dma((2, 2)),
            ]
            + [dma((PIECES,))] * 12,
            compiler_params=pltpu.CompilerParams(
                collective_id=0, has_side_effects=True, vmem_limit_bytes=48 << 20
            ),
            cost_estimate=pl.CostEstimate(
                flops=24 * rows * rows * width,
                bytes_accessed=12 * rows * width,
                transcendentals=4 * rows * rows,
            ),
        )(
            picture_vectors,
            caption_vectors,
            logit_multiplier.reshape(1, 1),
            logit_shift_term.reshape(1, 1),
        )

    placed = (P(("blk", "fold"), None), P(("blk", "fold"), None), P(), P())
    return jax.shard_map(
        shards,
        mesh=mesh,
        in_specs=placed,
        out_specs=(P(("blk", "fold"), None), P(("blk", "fold"), None)),
        check_vma=False,
    )
```

time: 191 us -> 94.6 us (0.50)
  the two profiles are of different devices: /device:TPU:246 before, /device:TPU:124 now
where the time goes in v1:
time: 94.6 us; the launch traced here: 94.3 us
  Pallas kernels  86 us (91%)
  local copies, waits for them, and re-layouts  6.45 us (7%)
  between operations  1.95 us (2%)
    pallas_call x1, Pallas kernels, shards(): pl.pallas_call(functools.partial(kernel, total, fold_size), out_shape=(ja...  86 us
    unnamed x8, local copies, waits for them, and re-layouts  6.45 us

profile of v1, /device:TPU:124, one launch (start us, length us, event | category | flops | bytes accessed | tf_op | source)
XLA Modules:
  0.0 94.3 jit_solution(13634041873466674784)
XLA Ops:
  1.9 0.0 copy-start
  1.9 1.3 %copy-done = bf16[512,1152]{1,0:T(8,128)(2,1)S(1)} copy-done((bf16[512,1152]{1,0:T(8,128)(2,1)S(1)}, bf16[512,1152]{1,0:T(8,128)(2,1)}, u32[]{:S(2)}) %copy-start) | copy-done | bytes 1179672
  3.2 0.0 copy-start.1
  3.2 1.3 %copy-done.1 = bf16[512,1152]{1,0:T(8,128)(2,1)S(1)} copy-done((bf16[512,1152]{1,0:T(8,128)(2,1)S(1)}, bf16[512,1152]{1,0:T(8,128)(2,1)}, u32[]{:S(2)}) %copy-start.1) | copy-done | bytes 1179672
  4.5 86.0 %shard_map.59 = (f32[512,1152]{1,0:T(8,128)S(1)}, f32[512,1152]{1,0:T(8,128)}) custom-call(bf16[512,1152]{1,0:T(8,128)(2,1)S(1)} %copy-done, bf16[512,1152]{1,0:T(8,128)(2,1)S(1)} %copy-done.1, f32[1,1]{1,0:T(1,128)} %bitcast.2.mult_ref, f32[1,1]{1,0:T(1,128)} %bitcast.3.shift_ref), custom_call_target="tpu_custom_call" | custom-call | flops 7247757312 | bytes 7077888 | tf_op jit(solution)/shard_map/pallas_call | solution.py:355
  90.4 0.0 copy-start.2
  90.4 1.4 %copy.10 = f32[512,1152]{1,0:T(8,128)} copy(f32[512,1152]{1,0:T(8,128)S(1)} %get-tuple-element.4) | data formatting | bytes 4718592
  91.8 1.1 %copy-done.2 = f32[512,1152]{1,0:T(8,128)S(1)} copy-done((f32[512,1152]{1,0:T(8,128)S(1)}, f32[512,1152]{1,0:T(8,128)}, u32[]{:S(2)}) %copy-start.2) | copy-done | bytes 2359320
  92.9 1.4 %copy.11 = f32[512,1152]{1,0:T(8,128)} copy(f32[512,1152]{1,0:T(8,128)S(1)} %copy-done.2) | data formatting | bytes 4718592
Async XLA Ops:
  1.9 1.3 %copy-start = (bf16[512,1152]{1,0:T(8,128)(2,1)S(1)}, bf16[512,1152]{1,0:T(8,128)(2,1)}, u32[]{:S(2)}) copy-start(bf16[512,1152]{1,0:T(8,128)(2,1)} %image_ref.1) | copy-start | bytes 3538948
  3.2 1.3 %copy-start.1 = (bf16[512,1152]{1,0:T(8,128)(2,1)S(1)}, bf16[512,1152]{1,0:T(8,128)(2,1)}, u32[]{:S(2)}) copy-start(bf16[512,1152]{1,0:T(8,128)(2,1)} %text_ref.1) | copy-start | bytes 3538948
  90.4 2.5 %copy-start.2 = (f32[512,1152]{1,0:T(8,128)S(1)}, f32[512,1152]{1,0:T(8,128)}, u32[]{:S(2)}) copy-start(f32[512,1152]{1,0:T(8,128)} %get-tuple-element.5) | copy-start | bytes 7077892

commit v2 on v1

v2 whole, which is shorter than its diff:
```python
import functools

import jax
import jax.numpy as jnp
from jax import lax
from jax.experimental import pallas as pl
from jax.experimental.pallas import tpu as pltpu
from jax.sharding import PartitionSpec as P

MESH = pl.DeviceIdType.MESH
PIECES = 8
PARTS = 4
HALVES = 2
OWN, PARTNER = 0, 1
A, M, X = 0, 1, 2


def kernel(
    total, fold_size, image_ref, text_ref, mult_ref, shift_ref, image_out, text_out,
    raw, imgs, texts, passing, scales, c_oa, c_px, c_om, c_pm, gi, gt, gx,
    gp_out, gm_out, gx_out, gp_in, gm_in, gx_in, stage,
    load_sem, store_sem, i_send, i_recv, m_send, m_recv, x_send, x_recv, r_send, r_recv, fw_send,
    gp_send, gp_recv, gm_send, gm_recv, gx_send, gx_recv,
):
    rows, width = raw.shape[1:]
    piece, part, half = rows // PIECES, rows // PARTS, rows // HALVES
    low = PIECES // HALVES
    per = PIECES // PARTS
    d = lax.axis_index("blk") * fold_size + lax.axis_index("fold")
    y = lax.rem(d, 4)
    odd = lax.rem(y, 2)
    x_slot = 2 * odd
    mult, shift = mult_ref[0, 0], shift_ref[0, 0]

    def device(number):
        number = lax.rem(number + total, total)
        return (number // fold_size, lax.rem(number, fold_size))

    def where(*values):
        picked = jnp.int32(values[0])
        for place in range(1, 4):
            picked = jnp.where(y == place, jnp.int32(values[place]), picked)
        return picked

    def span(f, size=None):
        size = piece if size is None else size
        return pl.ds(pl.multiple_of(f * size, size), size)

    partner = device(d + 1 - 2 * odd)

    def remote(src, dst, send, recv, target):
        return pltpu.make_async_remote_copy(
            src_ref=src, dst_ref=dst, send_sem=send, recv_sem=recv,
            device_id=target, device_id_type=MESH,
        )

    def i_copy(f):
        return remote(
            imgs.at[OWN, span(f)], imgs.at[PARTNER, span(f)], i_send.at[f], i_recv.at[f], partner
        )

    def m_copy(f, slot=A):
        return remote(
            texts.at[slot, span(f)], texts.at[M, span(f)], m_send.at[f], m_recv.at[f],
            device(d + where(3, 1, 3, -3)),
        )

    def x_copy(f):
        return remote(
            texts.at[A, span(f)], texts.at[X, span(f)], x_send.at[f], x_recv.at[f], device(d + 4)
        )

    def r_copy(f):
        return remote(
            texts.at[A, span(f)], passing.at[span(f)], r_send.at[f], r_recv.at[f], device(d - 3)
        )

    def r_forward(f):
        return remote(
            passing.at[span(f)], texts.at[M, span(f)], fw_send.at[f], m_recv.at[f], device(d + 4)
        )

    def gp_copy(f):
        return remote(gp_out.at[span(f)], gp_in.at[span(f)], gp_send.at[f], gp_recv.at[f], partner)

    def gm_copy(f):
        step = where(3, 1, -1, -3)
        step = jnp.where(jnp.logical_and(y == 0, f >= low), -1, step)
        return remote(
            gm_out.at[span(f)], gm_in.at[span(f)], gm_send.at[f], gm_recv.at[f], device(d + step)
        )

    def gx_copy(f, source):
        return remote(
            source.at[span(f)], gx_in.at[span(f)], gx_send.at[f], gx_recv.at[f], device(d - 4)
        )

    def load(which, f):
        source = (image_ref, text_ref)[which]
        return pltpu.make_async_copy(
            source.at[span(f)], raw.at[which, span(f)], load_sem.at[which, f]
        )

    barrier = pltpu.get_barrier_semaphore()
    near = {0: (1, 3, 4, -4, -1), 1: (-1, 1, 4, -4, -3), 2: (1, 3, -1, 4, -4), 3: (-1, -3, 4, -4, 1)}
    for place, offsets in near.items():

        @pl.when(y == place)
        def _():
            for offset in offsets:
                pl.semaphore_signal(
                    barrier, inc=1, device_id=device(d + offset), device_id_type=MESH
                )

    for f in range(PIECES):
        load(0, f).start()
        load(1, f).start()

    def normalize(which, f):
        load(which, f).wait()
        wide = raw[which, span(f), :].astype(jnp.float32)
        scale = 1.0 / jnp.sqrt(jnp.sum(wide * wide, axis=-1, keepdims=True) + 1e-06)
        scales[which, span(f), :] = jnp.broadcast_to(scale, (piece, scales.shape[-1]))
        (imgs, texts)[which][0, span(f), :] = (wide * scale).astype(jnp.bfloat16)

    def x_piece(f):
        return lax.rem(f + low, PIECES)

    def send_text(f):
        @pl.when(y < 3)
        def _():
            m_copy(f).start()

        @pl.when(jnp.logical_and(y == 3, f < low))
        def _():
            r_copy(f).start()

    normalize(0, 0)
    normalize(1, 0)
    pl.semaphore_wait(barrier, 5)
    i_copy(0).start()
    send_text(jnp.int32(0))

    @pl.loop(1, low)
    def _(f):
        normalize(0, f)
        normalize(1, f)
        i_copy(f).start()
        send_text(f)

    @pl.loop(low, PIECES)
    def _(f):
        normalize(1, f)
        send_text(f)

        @pl.when(odd == 1)
        def _():
            x_copy(f).start()

        normalize(0, f)
        i_copy(f).start()

    @pl.when(odd == 1)
    def _():
        for f in range(low):
            x_copy(f).start()

    def weigh(c_ref, image, i0, i_rows, text, t0, t_rows, diagonal=False):
        scores = lax.dot_general(
            imgs[image, pl.ds(i0, i_rows), :], texts[text, pl.ds(t0, t_rows), :],
            (((1,), (1,)), ((), ())), preferred_element_type=jnp.float32,
        )
        weights = jax.nn.sigmoid(mult * scores + shift)
        if diagonal:
            r = lax.broadcasted_iota(jnp.int32, weights.shape, 0) + i0
            c = lax.broadcasted_iota(jnp.int32, weights.shape, 1) + t0
            weights = jnp.where(r == c, weights - 1.0, weights)
        c_ref[pl.ds(i0, i_rows), pl.ds(t0, t_rows)] = (mult * weights).astype(jnp.bfloat16)

    def to_image(c_ref, c, text):
        return jnp.dot(
            c_ref[span(c, part), :], texts[text], preferred_element_type=jnp.float32
        )

    def to_text(c_ref, c, image):
        return lax.dot_general(
            c_ref[:, c * part : (c + 1) * part], imgs[image], (((0,), (0,)), ((), ())),
            preferred_element_type=jnp.float32,
        )

    weigh(c_oa, OWN, 0, half, A, 0, rows, diagonal=True)
    weigh(c_oa, OWN, half, half, A, 0, rows, diagonal=True)
    for c in range(PARTS):
        gi[span(c, part), :] = to_image(c_oa, c, A)
    for c in range(PARTS):
        gt[span(c, part), :] = to_text(c_oa, c, OWN)

    @pl.when(y == 0)
    def _():
        @pl.loop(0, low)
        def _(f):
            r_copy(f).wait_recv()
            r_forward(f).start()

    @pl.when(y == 3)
    def _():
        @pl.loop(0, low)
        def _(f):
            r_copy(f).wait_send()
            x_copy(f + low).wait_recv()
            m_copy(f + low, X).start()

    @pl.when(y == 1)
    def _():
        @pl.loop(low, PIECES)
        def _(f):
            x_copy(f).wait_recv()

    def wait_pair(first, past):
        @pl.loop(first, past)
        def _(f):
            i_copy(f).wait_recv()
            m_copy(f).wait_recv()

    wait_pair(0, low)
    weigh(c_om, OWN, 0, rows, M, 0, half)
    weigh(c_pm, PARTNER, 0, half, M, 0, half)
    weigh(c_px, PARTNER, 0, half, x_slot, half, half)

    wait_pair(low, PIECES)

    @pl.when(odd == 1)
    def _():
        @pl.loop(0, low)
        def _(f):
            x_copy(f).wait_recv()

    def give(value, out, copy, c):
        out[span(c, part), :] = value.astype(jnp.bfloat16)
        for f in range(c * per, (c + 1) * per):
            copy(f).start()

    def give_gp(c):
        give(to_image(c_px, c, x_slot) + to_image(c_pm, c, M), gp_out, gp_copy, c)

    def give_gm(c):
        give(to_text(c_om, c, OWN) + to_text(c_pm, c, PARTNER), gm_out, gm_copy, c)

    def give_gx(c):
        gx[span(c, part), :] = to_text(c_px, c, PARTNER)

        @pl.when(jnp.logical_or(y == 1, y == 3) if c >= PARTS // 2 else y == 1)
        def _():
            give(gx[span(c, part), :], gx_out, lambda f: gx_copy(f, gx_out), c)

    weigh(c_pm, PARTNER, half, half, M, 0, half)
    give_gm(0)
    weigh(c_pm, PARTNER, 0, half, M, half, half)
    weigh(c_px, PARTNER, 0, half, x_slot, 0, half)
    give_gp(0)
    give_gm(1)
    give_gp(1)
    weigh(c_px, PARTNER, half, half, x_slot, half, half)
    give_gx(2)
    give_gx(3)
    weigh(c_px, PARTNER, half, half, x_slot, 0, half)
    weigh(c_pm, PARTNER, half, half, M, half, half)
    weigh(c_om, OWN, 0, rows, M, half, half)
    give_gm(2)
    give_gp(2)
    give_gm(3)
    give_gp(3)
    give_gx(0)
    give_gx(1)

    def wide(ref, f):
        return ref[span(f), :].astype(jnp.float32)

    def relay(f):
        @pl.when(y == 2)
        def _():
            gm_copy(f).wait_recv()
            gx_copy(f, gm_in).start()

        @pl.when(jnp.logical_and(y == 3, f < low))
        def _():
            gm_copy(f).wait_recv()
            gx_out[span(f), :] = (gx[span(f), :] + wide(gm_in, f)).astype(jnp.bfloat16)
            gx_copy(f, gx_out).start()

    for c in range(PARTS):
        relay(jnp.int32(c))
        gi[span(c, part), :] += to_image(c_om, c, M)

        @pl.when(odd == 0)
        def _():
            gt[span(c, part), :] += gx[span(c, part), :]

    def store(which, f):
        target = (image_out, text_out)[which]
        slot = lax.rem(f, 2)
        return pltpu.make_async_copy(
            stage.at[which, slot], target.at[span(f)], store_sem.at[which, slot]
        )

    def finish(which, f, grad):
        scale = scales[which, span(f), :][:, :1]
        unit = raw[which, span(f), :].astype(jnp.float32) * scale
        inner = jnp.sum(unit * grad, axis=-1, keepdims=True)

        @pl.when(f >= 2)
        def _():
            store(which, f - 2).wait()

        stage[which, lax.rem(f, 2)] = scale * (grad - unit * inner)
        store(which, f).start()

    def finish_image(f):
        gp_copy(f).wait_recv()
        finish(0, f, gi[span(f), :] + wide(gp_in, f))

    def finish_text(f):
        @pl.when(jnp.logical_or(y < 2, jnp.logical_and(y == 3, f >= low)))
        def _():
            gm_copy(f).wait_recv()
            gt[span(f), :] += wide(gm_in, f)

        @pl.when(y > 0)
        def _():
            gx_copy(f, gx_out).wait_recv()
            gt[span(f), :] += wide(gx_in, f)

        finish(1, f, gt[span(f), :])

    @pl.loop(0, PIECES)
    def _(f):
        @pl.when(f >= PARTS)
        def _():
            relay(f)

        finish_image(f)

        @pl.when(f >= 1)
        def _():
            finish_text(f - 1)

    finish_text(jnp.int32(PIECES - 1))

    @pl.loop(0, PIECES)
    def _(f):
        i_copy(f).wait_send()
        gp_copy(f).wait_send()
        gm_copy(f).wait_send()

        @pl.when(jnp.logical_or(y < 3, f >= low))
        def _():
            m_copy(f).wait_send()

        @pl.when(jnp.logical_and(y == 0, f < low))
        def _():
            r_forward(f).wait_send()

        @pl.when(odd == 1)
        def _():
            x_copy(f).wait_send()

        @pl.when(y > 0)
        def _():
            gx_copy(f, gx_out).wait_send()

    for f in range(PIECES - 2, PIECES):
        store(0, jnp.int32(f)).wait()
        store(1, jnp.int32(f)).wait()


def solution(mesh):
    fold_size = mesh.shape["fold"]
    total = fold_size * mesh.shape["blk"]

    def shards(picture_vectors, caption_vectors, logit_multiplier, logit_shift_term):
        rows, width = picture_vectors.shape
        block = (rows, width)
        dma = pltpu.SemaphoreType.DMA
        return pl.pallas_call(
            functools.partial(kernel, total, fold_size),
            out_shape=(jax.ShapeDtypeStruct(block, jnp.float32),) * 2,
            in_specs=[pl.BlockSpec(memory_space=pl.ANY)] * 2
            + [pl.BlockSpec(memory_space=pltpu.SMEM)] * 2,
            out_specs=(pl.BlockSpec(memory_space=pl.ANY),) * 2,
            scratch_shapes=[
                pltpu.VMEM((2,) + block, jnp.bfloat16),
                pltpu.VMEM((2,) + block, jnp.bfloat16),
                pltpu.VMEM((3,) + block, jnp.bfloat16),
                pltpu.VMEM((rows // HALVES, width), jnp.bfloat16),
                pltpu.VMEM((2, rows, 128), jnp.float32),
            ]
            + [pltpu.VMEM((rows, rows), jnp.bfloat16)] * 4
            + [pltpu.VMEM(block, jnp.float32)] * 3
            + [pltpu.VMEM(block, jnp.bfloat16)] * 6
            + [
                pltpu.VMEM((2, 2, rows // PIECES, width), jnp.float32),
                dma((2, PIECES)),
                dma((2, 2)),
            ]
            + [dma((PIECES,))] * 15,
            compiler_params=pltpu.CompilerParams(
                collective_id=0, has_side_effects=True, vmem_limit_bytes=58 << 20
            ),
            cost_estimate=pl.CostEstimate(
                flops=24 * rows * rows * width,
                bytes_accessed=12 * rows * width,
                transcendentals=4 * rows * rows,
            ),
        )(
            picture_vectors,
            caption_vectors,
            logit_multiplier.reshape(1, 1),
            logit_shift_term.reshape(1, 1),
        )

    placed = (P(("blk", "fold"), None), P(("blk", "fold"), None), P(), P())
    return jax.shard_map(
        shards,
        mesh=mesh,
        in_specs=placed,
        out_specs=(P(("blk", "fold"), None), P(("blk", "fold"), None)),
        check_vma=False,
    )
```

time: 94.6 us -> 76.2 us (0.81)
  the two profiles are of different devices: /device:TPU:124 before, /device:TPU:127 now
where the time goes in v2:
time: 76.2 us; the launch traced here: 75.4 us
  Pallas kernels  68.7 us (90%)
  local copies, waits for them, and re-layouts  4.78 us (6%)
  between operations  1.94 us (3%)
    pallas_call x1, Pallas kernels, shards(): pl.pallas_call(functools.partial(kernel, total, fold_size), out_shape=(ja...  68.7 us
    unnamed x4, local copies, waits for them, and re-layouts  4.78 us

profile of v2, /device:TPU:127, one launch (start us, length us, event | category | flops | bytes accessed | tf_op | source)
XLA Modules:
  0.0 75.4 jit_solution(827470074236493247)
XLA Ops:
  1.9 68.7 %shard_map.59 = (f32[512,1152]{1,0:T(8,128)}, f32[512,1152]{1,0:T(8,128)}) custom-call(bf16[512,1152]{1,0:T(8,128)(2,1)} %image_ref.1, bf16[512,1152]{1,0:T(8,128)(2,1)} %text_ref.1, f32[1,1]{1,0:T(1,128)} %bitcast.2.mult_ref, f32[1,1]{1,0:T(1,128)} %bitcast.3.shift_ref), custom_call_target="tpu_custom_call" | custom-call | flops 7247757312 | bytes 7077888 | tf_op jit(solution)/shard_map/pallas_call | solution.py:384
  70.6 0.0 copy-start
  70.7 3.4 %copy.10 = f32[512,1152]{1,0:T(8,128)} copy(f32[512,1152]{1,0:T(8,128)} %get-tuple-element.4) | data formatting | bytes 4718592
  74.0 0.0 copy-done
  74.0 1.4 %copy.11 = f32[512,1152]{1,0:T(8,128)} copy(f32[512,1152]{1,0:T(8,128)S(1)} %copy-done) | data formatting | bytes 4718592
Async XLA Ops:
  70.6 3.4 %copy-start = (f32[512,1152]{1,0:T(8,128)S(1)}, f32[512,1152]{1,0:T(8,128)}, u32[]{:S(2)}) copy-start(f32[512,1152]{1,0:T(8,128)} %get-tuple-element.5) | copy-start | bytes 7077892

commit v3 on v2

v3 whole, which is shorter than its diff:
```python
import functools

import jax
import jax.numpy as jnp
from jax import lax
from jax.experimental import pallas as pl
from jax.experimental.pallas import tpu as pltpu
from jax.sharding import PartitionSpec as P

MESH = pl.DeviceIdType.MESH
PIECES = 8
PARTS = 4
LATE = 7
HALVES = 2
OWN, PARTNER = 0, 1
A, M, X = 0, 1, 2


def kernel(
    total, fold_size, image_ref, text_ref, mult_ref, shift_ref, image_out, text_out,
    raw, imgs, texts, passing, scales, c_oa, c_px, c_om, c_pm, gi, gt, early_m, early_x, early_p,
    gp_out, gm_out, gx_out, gp_in, gm_in, gx_in,
    load_sem, i_send, i_recv, m_send, m_recv, x_send, x_recv, r_send, r_recv, fw_send,
    gp_send, gp_recv, gm_send, gm_recv, gx_send, gx_recv,
):
    rows, width = raw.shape[1:]
    piece, part, half = rows // PIECES, rows // PARTS, rows // HALVES
    low = PIECES // HALVES
    low_part = PARTS // HALVES
    per = PIECES // PARTS
    d = lax.axis_index("blk") * fold_size + lax.axis_index("fold")
    y = lax.rem(d, 4)
    odd = lax.rem(y, 2)
    x_slot = 2 * odd
    mult, shift = mult_ref[0, 0], shift_ref[0, 0]

    def device(number):
        number = lax.rem(number + total, total)
        return (number // fold_size, lax.rem(number, fold_size))

    def where(*values):
        picked = jnp.int32(values[0])
        for place in range(1, 4):
            picked = jnp.where(y == place, jnp.int32(values[place]), picked)
        return picked

    def span(f, size=None):
        size = piece if size is None else size
        return pl.ds(pl.multiple_of(f * size, size), size)

    partner = device(d + 1 - 2 * odd)

    def remote(src, dst, send, recv, target):
        return pltpu.make_async_remote_copy(
            src_ref=src, dst_ref=dst, send_sem=send, recv_sem=recv,
            device_id=target, device_id_type=MESH,
        )

    def i_copy(f):
        return remote(
            imgs.at[OWN, span(f, part)], imgs.at[PARTNER, span(f, part)], i_send.at[f], i_recv.at[f], partner
        )

    def m_copy(f, slot=A):
        return remote(
            texts.at[slot, span(f, part)], texts.at[M, span(f, part)], m_send.at[f], m_recv.at[f],
            device(d + where(3, 1, 3, -3)),
        )

    def x_copy(f):
        return remote(
            texts.at[A, span(f, part)], texts.at[X, span(f, part)], x_send.at[f], x_recv.at[f], device(d + 4)
        )

    def r_copy(f):
        return remote(
            texts.at[A, span(f, part)], passing.at[span(f, part)], r_send.at[f], r_recv.at[f], device(d - 3)
        )

    def r_forward(f):
        return remote(
            passing.at[span(f, part)], texts.at[M, span(f, part)], fw_send.at[f], m_recv.at[f], device(d + 4)
        )

    def gp_copy(f):
        return remote(gp_out.at[span(f, part)], gp_in.at[span(f, part)], gp_send.at[f], gp_recv.at[f], partner)

    straight = where(low, LATE, PIECES, PIECES)
    straight_in = where(PIECES, PIECES, LATE, low)

    def gm_copy(f):
        step = jnp.where(f >= straight, where(-1, -3, -1, -3), where(3, 1, -1, -3))
        return remote(
            gm_out.at[span(f)], gm_in.at[span(f)], gm_send.at[f], gm_recv.at[f], device(d + step)
        )

    def gx_copy(f, source):
        return remote(
            source.at[span(f)], gx_in.at[span(f)], gx_send.at[f], gx_recv.at[f], device(d - 4)
        )

    def load(which, f):
        source = (image_ref, text_ref)[which]
        return pltpu.make_async_copy(
            source.at[span(f, part)], raw.at[which, span(f, part)], load_sem.at[which, f]
        )

    barrier = pltpu.get_barrier_semaphore()
    near = {0: (1, 3, 4, -4, -1), 1: (-1, 1, 4, -4, -3), 2: (1, 3, -1, 4, -4), 3: (-1, -3, 4, -4, 1)}
    for place, offsets in near.items():

        @pl.when(y == place)
        def _():
            for offset in offsets:
                pl.semaphore_signal(
                    barrier, inc=1, device_id=device(d + offset), device_id_type=MESH
                )

    for f in range(PARTS):
        load(0, f).start()
        load(1, f).start()

    def normalize(which, f):
        load(which, f).wait()
        here = span(f, part)
        wide = raw[which, here, :].astype(jnp.float32)
        scale = 1.0 / jnp.sqrt(jnp.sum(wide * wide, axis=-1, keepdims=True) + 1e-06)
        scales[which, here, :] = jnp.broadcast_to(scale, (part, scales.shape[-1]))
        (imgs, texts)[which][0, here, :] = (wide * scale).astype(jnp.bfloat16)

    def send_text(f):
        @pl.when(y < 3)
        def _():
            m_copy(f).start()

        if f < low_part:

            @pl.when(y == 3)
            def _():
                r_copy(f).start()

    def send_x(f):
        @pl.when(odd == 1)
        def _():
            x_copy(f).start()

    normalize(0, 0)
    normalize(1, 0)
    pl.semaphore_wait(barrier, 5)
    i_copy(0).start()
    send_text(0)
    normalize(1, low_part)
    send_x(low_part)
    for f in range(1, PARTS):
        normalize(0, f)
        i_copy(f).start()
        if f != low_part:
            normalize(1, f)
        send_text(f)
        if f > low_part:
            send_x(f)
    for f in range(low_part):
        send_x(f)

    def weigh(c_ref, image, i0, i_rows, text, t0, t_rows, diagonal=False):
        scores = lax.dot_general(
            imgs[image, pl.ds(i0, i_rows), :], texts[text, pl.ds(t0, t_rows), :],
            (((1,), (1,)), ((), ())), preferred_element_type=jnp.float32,
        )
        weights = jax.nn.sigmoid(mult * scores + shift)
        if diagonal:
            r = lax.broadcasted_iota(jnp.int32, weights.shape, 0) + i0
            c = lax.broadcasted_iota(jnp.int32, weights.shape, 1) + t0
            weights = jnp.where(r == c, weights - 1.0, weights)
        c_ref[pl.ds(i0, i_rows), pl.ds(t0, t_rows)] = (mult * weights).astype(jnp.bfloat16)

    def to_image(c_ref, c, text, start=0, size=rows):
        return jnp.dot(
            c_ref[span(c, part), start : start + size], texts[text, start : start + size, :],
            preferred_element_type=jnp.float32,
        )

    def x_to_image(c, start=0, size=rows):
        return jnp.dot(
            c_px[span(c, part), start : start + size], texts[x_slot, start : start + size, :],
            preferred_element_type=jnp.float32,
        )

    def to_text(c_ref, c, image, start=0, size=rows):
        return lax.dot_general(
            c_ref[start : start + size, c * part : (c + 1) * part],
            imgs[image, start : start + size, :],
            (((0,), (0,)), ((), ())), preferred_element_type=jnp.float32,
        )

    weigh(c_oa, OWN, 0, half, A, 0, rows, diagonal=True)
    weigh(c_oa, OWN, half, half, A, 0, rows, diagonal=True)
    for c in range(PARTS):
        gi[span(c, part), :] = to_image(c_oa, c, A)
    for c in range(PARTS):
        gt[span(c, part), :] = to_text(c_oa, c, OWN)

    @pl.when(y == 0)
    def _():
        for f in range(low_part):
            r_copy(f).wait_recv()
            r_forward(f).start()

    @pl.when(y == 3)
    def _():
        for f in range(low_part):
            r_copy(f).wait_send()
            x_copy(f + low_part).wait_recv()
            m_copy(f + low_part, X).start()

    @pl.when(y == 1)
    def _():
        for f in range(low_part, PARTS):
            x_copy(f).wait_recv()

    def wait_pair(first, past):
        for f in range(first, past):
            i_copy(f).wait_recv()
            m_copy(f).wait_recv()

    wait_pair(0, low_part)
    weigh(c_om, OWN, 0, rows, M, 0, half)
    weigh(c_pm, PARTNER, 0, half, M, 0, half)
    weigh(c_px, PARTNER, 0, half, x_slot, half, half)
    for c in range(low_part):
        early_m[span(c, part), :] = to_text(c_om, c, OWN) + to_text(c_pm, c, PARTNER, 0, half)
        early_x[span(c, part), :] = to_text(c_px, c + low_part, PARTNER, 0, half)
        early_p[span(c, part), :] = x_to_image(c, half, half) + to_image(c_pm, c, M, 0, half)
    for c in range(PARTS):
        gi[span(c, part), :] += to_image(c_om, c, M, 0, half)

    wait_pair(low_part, PARTS)

    @pl.when(odd == 1)
    def _():
        for f in range(low_part):
            x_copy(f).wait_recv()

    def give_gp(c, value):
        gp_out[span(c, part), :] = value.astype(jnp.bfloat16)
        gp_copy(c).start()

    def give(value, out, copy, c):
        out[span(c, part), :] = value.astype(jnp.bfloat16)
        for f in range(c * per, (c + 1) * per):
            copy(f).start()

    def give_gm(c, value):
        gm_out[span(c, part), :] = value.astype(jnp.bfloat16)

        @pl.when(jnp.logical_or(y > 0, c < low_part))
        def _():
            for f in range(c * per, (c + 1) * per):
                gm_copy(f).start()

    def give_gx(c, value):
        give(value, gx_out, lambda f: gx_copy(f, gx_out), c)

    def late_m(c):
        return early_m[span(c, part), :] + to_text(c_pm, c, PARTNER, half, half)

    def late_x(c):
        return early_x[span(c - low_part, part), :] + to_text(c_px, c, PARTNER, half, half)

    def late_p(c):
        return early_p[span(c, part), :] + x_to_image(c, 0, half) + to_image(c_pm, c, M, half, half)

    weigh(c_pm, PARTNER, half, half, M, 0, half)
    give_gm(0, late_m(0))
    weigh(c_px, PARTNER, half, half, x_slot, half, half)

    @pl.when(odd == 1)
    def _():
        give_gx(low_part, late_x(low_part))

    weigh(c_pm, PARTNER, 0, half, M, half, half)
    weigh(c_px, PARTNER, 0, half, x_slot, 0, half)
    give_gp(0, late_p(0))
    for c in range(1, low_part):
        give_gm(c, late_m(c))
        give_gp(c, late_p(c))

        @pl.when(odd == 1)
        def _():
            give_gx(low_part + c, late_x(low_part + c))

    weigh(c_om, OWN, 0, rows, M, half, half)
    weigh(c_pm, PARTNER, half, half, M, half, half)
    weigh(c_px, PARTNER, half, half, x_slot, 0, half)
    for c in range(low_part, PARTS):
        give_gm(c, to_text(c_om, c, OWN) + to_text(c_pm, c, PARTNER))
        give_gp(c, x_to_image(c) + to_image(c_pm, c, M))

    @pl.when(y == 1)
    def _():
        for c in range(low_part):
            give_gx(c, to_text(c_px, c, PARTNER))

    @pl.when(y == 3)
    def _():
        for c in range(low_part):
            early_x[span(c, part), :] = to_text(c_px, c, PARTNER)

    def wide(ref, f):
        return ref[span(f), :].astype(jnp.float32)

    def relay(f):
        @pl.when(jnp.logical_and(y == 2, f < LATE))
        def _():
            gm_copy(f).wait_recv()
            gx_copy(f, gm_in).start()

        @pl.when(jnp.logical_and(y == 3, f < low))
        def _():
            gm_copy(f).wait_recv()
            gx_out[span(f), :] = (early_x[span(f), :] + wide(gm_in, f)).astype(jnp.bfloat16)
            gx_copy(f, gx_out).start()

    for c in range(PARTS):
        relay(jnp.int32(c))
        gi[span(c, part), :] += to_image(c_om, c, M, half, half)

        @pl.when(odd == 0)
        def _():
            gt[span(c, part), :] += to_text(c_px, c, PARTNER)

    @pl.when(y == 0)
    def _():
        for f in range(low):
            gm_copy(f).wait_send()
            gm_copy(f + low).start()

    def finish(which, f, grad):
        scale = scales[which, span(f), :][:, :1]
        unit = raw[which, span(f), :].astype(jnp.float32) * scale
        inner = jnp.sum(unit * grad, axis=-1, keepdims=True)

        (image_out, text_out)[which][span(f), :] = scale * (grad - unit * inner)

    def finish_image(f):
        @pl.when(lax.rem(f, per) == 0)
        def _():
            gp_copy(f // per).wait_recv()

        finish(0, f, gi[span(f), :] + wide(gp_in, f))

    def finish_text(f):
        @pl.when(jnp.logical_or(y < 2, f >= straight_in))
        def _():
            gm_copy(f).wait_recv()
            gt[span(f), :] += wide(gm_in, f)

        @pl.when(jnp.logical_and(y > 0, jnp.logical_or(y != 2, f < LATE)))
        def _():
            gx_copy(f, gx_out).wait_recv()
            gt[span(f), :] += wide(gx_in, f)

        finish(1, f, gt[span(f), :])

    @pl.loop(0, PIECES)
    def _(f):
        @pl.when(f >= PARTS)
        def _():
            relay(f)

        finish_image(f)

        @pl.when(f >= 1)
        def _():
            finish_text(f - 1)

    finish_text(jnp.int32(PIECES - 1))

    @pl.loop(0, PARTS)
    def _(f):
        i_copy(f).wait_send()
        gp_copy(f).wait_send()

        @pl.when(jnp.logical_or(y < 3, f >= low_part))
        def _():
            m_copy(f).wait_send()

        @pl.when(jnp.logical_and(y == 0, f < low_part))
        def _():
            r_forward(f).wait_send()

        @pl.when(odd == 1)
        def _():
            x_copy(f).wait_send()

    @pl.loop(0, PIECES)
    def _(f):
        @pl.when(jnp.logical_or(y > 0, f >= low))
        def _():
            gm_copy(f).wait_send()

        @pl.when(jnp.logical_and(y > 0, jnp.logical_or(y != 2, f < LATE)))
        def _():
            gx_copy(f, gx_out).wait_send()


def store(image_ref, text_ref, image_out, text_out, sem):
    size = image_ref.shape[0] // PIECES

    def copy(which, f):
        source, target = ((image_ref, image_out), (text_ref, text_out))[which]
        here = pl.ds(f * size, size)
        return pltpu.make_async_copy(source.at[here], target.at[here], sem.at[which, f])

    for f in range(PIECES):
        copy(0, f).start()
        copy(1, f).start()
    for f in range(PIECES):
        copy(0, f).wait()
        copy(1, f).wait()


def solution(mesh):
    fold_size = mesh.shape["fold"]
    total = fold_size * mesh.shape["blk"]

    def shards(picture_vectors, caption_vectors, logit_multiplier, logit_shift_term):
        rows, width = picture_vectors.shape
        block = (rows, width)
        dma = pltpu.SemaphoreType.DMA
        grads = pl.pallas_call(
            functools.partial(kernel, total, fold_size),
            out_shape=(jax.ShapeDtypeStruct(block, jnp.float32),) * 2,
            in_specs=[pl.BlockSpec(memory_space=pl.ANY)] * 2
            + [pl.BlockSpec(memory_space=pltpu.SMEM)] * 2,
            out_specs=(pl.BlockSpec(memory_space=pltpu.VMEM),) * 2,
            scratch_shapes=[
                pltpu.VMEM((2,) + block, jnp.bfloat16),
                pltpu.VMEM((2,) + block, jnp.bfloat16),
                pltpu.VMEM((3,) + block, jnp.bfloat16),
                pltpu.VMEM((rows // HALVES, width), jnp.bfloat16),
                pltpu.VMEM((2, rows, 128), jnp.float32),
            ]
            + [pltpu.VMEM((rows, rows), jnp.bfloat16)] * 4
            + [pltpu.VMEM(block, jnp.float32)] * 2
            + [pltpu.VMEM((rows // HALVES, width), jnp.float32)] * 3
            + [pltpu.VMEM(block, jnp.bfloat16)] * 6
            + [
                dma((2, PIECES)),
            ]
            + [dma((PIECES,))] * 15,
            compiler_params=pltpu.CompilerParams(
                collective_id=0, has_side_effects=True, vmem_limit_bytes=40 << 20
            ),
            cost_estimate=pl.CostEstimate(
                flops=24 * rows * rows * width,
                bytes_accessed=12 * rows * width,
                transcendentals=4 * rows * rows,
            ),
        )(
            pltpu.with_memory_space_constraint(picture_vectors, pltpu.HBM),
            pltpu.with_memory_space_constraint(caption_vectors, pltpu.HBM),
            logit_multiplier.reshape(1, 1),
            logit_shift_term.reshape(1, 1),
        )
        return pl.pallas_call(
            store,
            out_shape=(jax.ShapeDtypeStruct(block, jnp.float32),) * 2,
            in_specs=[pl.BlockSpec(memory_space=pl.ANY)] * 2,
            out_specs=(pl.BlockSpec(memory_space=pl.ANY),) * 2,
            scratch_shapes=[dma((2, PIECES))],
            compiler_params=pltpu.CompilerParams(vmem_limit_bytes=1 << 20),
        )(*grads)

    placed = (P(("blk", "fold"), None), P(("blk", "fold"), None), P(), P())
    return jax.shard_map(
        shards,
        mesh=mesh,
        in_specs=placed,
        out_specs=(P(("blk", "fold"), None), P(("blk", "fold"), None)),
        check_vma=False,
    )
```

time: 76.2 us -> 71.3 us (0.936)
  local copies, waits for them, and re-layouts: 4.78 us -> 0 us
    unnamed x4 -> x0, local copies, waits for them, and re-layouts: 4.78 us -> none
    pallas_call x1, Pallas kernels: 68.7 us -> 65.8 us  [shards(): pl.pallas_call(functools.partial(kernel, total, fold_size), out_shape=(ja...]
    pallas_call x0 -> x1, Pallas kernels: none -> 2.31 us  [shards(): pl.pallas_call(store, out_shape=(jax.ShapeDtypeStruct(block, jnp.float32)...]
where the time goes in v3:
time: 71.3 us; the launch traced here: 70.1 us
  Pallas kernels  68.1 us (96%)
  between operations  1.93 us (3%)
    pallas_call x1, Pallas kernels, shards(): pl.pallas_call(functools.partial(kernel, total, fold_size), out_shape=(ja...  65.8 us
    pallas_call x1, Pallas kernels, shards(): pl.pallas_call(store, out_shape=(jax.ShapeDtypeStruct(block, jnp.float32)...  2.31 us

profile of v3, /device:TPU:127, one launch (start us, length us, event | category | flops | bytes accessed | tf_op | source)
XLA Modules:
  0.0 70.1 jit_solution(10963734882199296759)
XLA Ops:
  1.9 65.8 %shard_map.59 = (f32[512,1152]{1,0:T(8,128)S(1)}, f32[512,1152]{1,0:T(8,128)S(1)}) custom-call(bf16[512,1152]{1,0:T(8,128)(2,1)} %image_ref.1, bf16[512,1152]{1,0:T(8,128)(2,1)} %text_ref.1, f32[1,1]{1,0:T(1,128)} %bitcast.2.mult_ref, f32[1,1]{1,0:T(1,128)} %bitcast.3.shift_ref), custom_call_target="tpu_custom_call" | custom-call | flops 7247757312 | bytes 7077888 | tf_op jit(solution)/shard_map/pallas_call | solution.py:431
  67.7 2.3 %shard_map.60 = (f32[512,1152]{1,0:T(8,128)}, f32[512,1152]{1,0:T(8,128)}) custom-call(f32[512,1152]{1,0:T(8,128)S(1)} %get-tuple-element.4.image_ref, f32[512,1152]{1,0:T(8,128)S(1)} %get-tuple-element.5.text_ref), custom_call_target="tpu_custom_call" | custom-call | tf_op jit(solution)/shard_map/pallas_call | solution.py:466

commit v4 on v3

--- a/solution.py
+++ b/solution.py
@@ -11,6 +11,8 @@
 PIECES = 8
 PARTS = 4
 LATE = 7
+LAG = 3
+STORES = 2
 HALVES = 2
 OWN, PARTNER = 0, 1
 A, M, X = 0, 1, 2
@@ -85,13 +87,18 @@
     def gp_copy(f):
         return remote(gp_out.at[span(f, part)], gp_in.at[span(f, part)], gp_send.at[f], gp_recv.at[f], partner)
 
-    straight = where(low, LATE, PIECES, PIECES)
-    straight_in = where(PIECES, PIECES, LATE, low)
+    n_handed = low
+    straight_in = where(PIECES, PIECES, LATE, n_handed)
 
     def gm_copy(f):
-        step = jnp.where(f >= straight, where(-1, -3, -1, -3), where(3, 1, -1, -3))
+        step = jnp.where(jnp.logical_and(y == 1, f >= LATE), -3, where(-1, 1, -1, -3))
         return remote(
             gm_out.at[span(f)], gm_in.at[span(f)], gm_send.at[f], gm_recv.at[f], device(d + step)
+        )
+
+    def hand_copy(f):
+        return remote(
+            gm_out.at[span(f)], passing.at[span(f)], gm_send.at[f], r_recv.at[f], device(d + 3)
         )
 
     def gx_copy(f, source):
@@ -145,9 +152,9 @@
             x_copy(f).start()
 
     normalize(0, 0)
-    normalize(1, 0)
     pl.semaphore_wait(barrier, 5)
     i_copy(0).start()
+    normalize(1, 0)
     send_text(0)
     normalize(1, low_part)
     send_x(low_part)
@@ -218,12 +225,9 @@
         for f in range(low_part, PARTS):
             x_copy(f).wait_recv()
 
-    def wait_pair(first, past):
-        for f in range(first, past):
-            i_copy(f).wait_recv()
-            m_copy(f).wait_recv()
-
-    wait_pair(0, low_part)
+    for f in range(low_part):
+        i_copy(f).wait_recv()
+        m_copy(f).wait_recv()
     weigh(c_om, OWN, 0, rows, M, 0, half)
     weigh(c_pm, PARTNER, 0, half, M, 0, half)
     weigh(c_px, PARTNER, 0, half, x_slot, half, half)
@@ -234,13 +238,6 @@
     for c in range(PARTS):
         gi[span(c, part), :] += to_image(c_om, c, M, 0, half)
 
-    wait_pair(low_part, PARTS)
-
-    @pl.when(odd == 1)
-    def _():
-        for f in range(low_part):
-            x_copy(f).wait_recv()
-
     def give_gp(c, value):
         gp_out[span(c, part), :] = value.astype(jnp.bfloat16)
         gp_copy(c).start()
@@ -253,9 +250,15 @@
     def give_gm(c, value):
         gm_out[span(c, part), :] = value.astype(jnp.bfloat16)
 
-        @pl.when(jnp.logical_or(y > 0, c < low_part))
-        def _():
-            for f in range(c * per, (c + 1) * per):
+        for f in range(c * per, (c + 1) * per):
+            by_hand = jnp.logical_and(y == 0, f < n_handed)
+
+            @pl.when(by_hand)
+            def _():
+                hand_copy(f).start()
+
+            @pl.when(jnp.logical_not(by_hand))
+            def _():
                 gm_copy(f).start()
 
     def give_gx(c, value):
@@ -270,6 +273,8 @@
     def late_p(c):
         return early_p[span(c, part), :] + x_to_image(c, 0, half) + to_image(c_pm, c, M, half, half)
 
+    for f in range(low_part, PARTS):
+        i_copy(f).wait_recv()
     weigh(c_pm, PARTNER, half, half, M, 0, half)
     give_gm(0, late_m(0))
     weigh(c_px, PARTNER, half, half, x_slot, half, half)
@@ -277,6 +282,14 @@
     @pl.when(odd == 1)
     def _():
         give_gx(low_part, late_x(low_part))
+
+    for f in range(low_part, PARTS):
+        m_copy(f).wait_recv()
+
+    @pl.when(odd == 1)
+    def _():
+        for f in range(low_part):
+            x_copy(f).wait_recv()
 
     weigh(c_pm, PARTNER, 0, half, M, half, half)
     weigh(c_px, PARTNER, 0, half, x_slot, 0, half)
@@ -296,15 +309,17 @@
         give_gm(c, to_text(c_om, c, OWN) + to_text(c_pm, c, PARTNER))
         give_gp(c, x_to_image(c) + to_image(c_pm, c, M))
 
-    @pl.when(y == 1)
+    @pl.when(odd == 1)
     def _():
         for c in range(low_part):
-            give_gx(c, to_text(c_px, c, PARTNER))
-
-    @pl.when(y == 3)
-    def _():
-        for c in range(low_part):
-            early_x[span(c, part), :] = to_text(c_px, c, PARTNER)
+            value = to_text(c_px, c, PARTNER)
+            early_x[span(c, part), :] = value
+            gx_out[span(c, part), :] = value.astype(jnp.bfloat16)
+            for f in range(c * per, (c + 1) * per):
+
+                @pl.when(jnp.logical_or(y == 1, f >= n_handed))
+                def _():
+                    gx_copy(f, gx_out).start()
 
     def wide(ref, f):
         return ref[span(f), :].astype(jnp.float32)
@@ -315,10 +330,10 @@
             gm_copy(f).wait_recv()
             gx_copy(f, gm_in).start()
 
-        @pl.when(jnp.logical_and(y == 3, f < low))
-        def _():
-            gm_copy(f).wait_recv()
-            gx_out[span(f), :] = (early_x[span(f), :] + wide(gm_in, f)).astype(jnp.bfloat16)
+        @pl.when(jnp.logical_and(y == 3, f < n_handed))
+        def _():
+            hand_copy(f).wait_recv()
+            gx_out[span(f), :] = (early_x[span(f), :] + wide(passing, f)).astype(jnp.bfloat16)
             gx_copy(f, gx_out).start()
 
     for c in range(PARTS):
@@ -328,12 +343,6 @@
         @pl.when(odd == 0)
         def _():
             gt[span(c, part), :] += to_text(c_px, c, PARTNER)
-
-    @pl.when(y == 0)
-    def _():
-        for f in range(low):
-            gm_copy(f).wait_send()
-            gm_copy(f + low).start()
 
     def finish(which, f, grad):
         scale = scales[which, span(f), :][:, :1]
@@ -362,19 +371,19 @@
 
         finish(1, f, gt[span(f), :])
 
-    @pl.loop(0, PIECES)
+    def text_order(k):
+        return jnp.where(y == 2, k, lax.div(k, 2) + low * lax.rem(k, 2))
+
+    @pl.loop(0, PIECES + LAG)
     def _(f):
-        @pl.when(f >= PARTS)
+        @pl.when(jnp.logical_and(f >= PARTS, f < PIECES))
         def _():
             relay(f)
 
-        finish_image(f)
-
-        @pl.when(f >= 1)
-        def _():
-            finish_text(f - 1)
-
-    finish_text(jnp.int32(PIECES - 1))
+        @pl.when(f >= LAG)
+        def _():
+            finish_image(f - LAG)
+            finish_text(text_order(f - LAG))
 
     @pl.loop(0, PARTS)
     def _(f):
@@ -395,9 +404,7 @@
 
     @pl.loop(0, PIECES)
     def _(f):
-        @pl.when(jnp.logical_or(y > 0, f >= low))
-        def _():
-            gm_copy(f).wait_send()
+        gm_copy(f).wait_send()
 
         @pl.when(jnp.logical_and(y > 0, jnp.logical_or(y != 2, f < LATE)))
         def _():
@@ -405,17 +412,17 @@
 
 
 def store(image_ref, text_ref, image_out, text_out, sem):
-    size = image_ref.shape[0] // PIECES
+    size = image_ref.shape[0] // STORES
 
     def copy(which, f):
         source, target = ((image_ref, image_out), (text_ref, text_out))[which]
         here = pl.ds(f * size, size)
         return pltpu.make_async_copy(source.at[here], target.at[here], sem.at[which, f])
 
-    for f in range(PIECES):
+    for f in range(STORES):
         copy(0, f).start()
         copy(1, f).start()
-    for f in range(PIECES):
+    for f in range(STORES):
         copy(0, f).wait()
         copy(1, f).wait()
 
@@ -468,7 +475,7 @@
             out_shape=(jax.ShapeDtypeStruct(block, jnp.float32),) * 2,
             in_specs=[pl.BlockSpec(memory_space=pl.ANY)] * 2,
             out_specs=(pl.BlockSpec(memory_space=pl.ANY),) * 2,
-            scratch_shapes=[dma((2, PIECES))],
+            scratch_shapes=[dma((2, STORES))],
             compiler_params=pltpu.CompilerParams(vmem_limit_bytes=1 << 20),
         )(*grads)
 

time: 71.3 us -> 70.6 us (level); the launches traced: 70.1 us -> 70.1 us
  no operation moved by 1% of the time
where the time goes in v4:
time: 70.6 us; the launch traced here: 70.1 us
  Pallas kernels  68.2 us (97%)
  between operations  1.93 us (3%)
    pallas_call x1, Pallas kernels, shards(): pl.pallas_call(functools.partial(kernel, total, fold_size), out_shape=(ja...  66 us
    pallas_call x1, Pallas kernels, shards(): pl.pallas_call(store, out_shape=(jax.ShapeDtypeStruct(block, jnp.float32)...  2.22 us

profile of v4, /device:TPU:127, one launch (start us, length us, event | category | flops | bytes accessed | tf_op | source)
XLA Modules:
  0.0 70.1 jit_solution(12472283720932993200)
XLA Ops:
  1.9 66.0 %shard_map.59 = (f32[512,1152]{1,0:T(8,128)S(1)}, f32[512,1152]{1,0:T(8,128)S(1)}) custom-call(bf16[512,1152]{1,0:T(8,128)(2,1)} %image_ref.1, bf16[512,1152]{1,0:T(8,128)(2,1)} %text_ref.1, f32[1,1]{1,0:T(1,128)} %bitcast.2.mult_ref, f32[1,1]{1,0:T(1,128)} %bitcast.3.shift_ref), custom_call_target="tpu_custom_call" | custom-call | flops 7247757312 | bytes 7077888 | tf_op jit(solution)/shard_map/pallas_call | solution.py:438
  67.9 2.2 %shard_map.60 = (f32[512,1152]{1,0:T(8,128)}, f32[512,1152]{1,0:T(8,128)}) custom-call(f32[512,1152]{1,0:T(8,128)S(1)} %get-tuple-element.4.image_ref, f32[512,1152]{1,0:T(8,128)S(1)} %get-tuple-element.5.text_ref), custom_call_target="tpu_custom_call" | custom-call | tf_op jit(solution)/shard_map/pallas_call | solution.py:473

commit v5 on v4

--- a/solution.py
+++ b/solution.py
@@ -257,7 +257,7 @@
             def _():
                 hand_copy(f).start()
 
-            @pl.when(jnp.logical_not(by_hand))
+            @pl.when(y > (1 if f == LATE else 0))
             def _():
                 gm_copy(f).start()
 
@@ -344,6 +344,12 @@
         def _():
             gt[span(c, part), :] += to_text(c_px, c, PARTNER)
 
+    @pl.when(y == 0)
+    def _():
+        for f in range(n_handed):
+            hand_copy(f).wait_send()
+            gm_copy(f + n_handed).start()
+
     def finish(which, f, grad):
         scale = scales[which, span(f), :][:, :1]
         unit = raw[which, span(f), :].astype(jnp.float32) * scale
@@ -380,6 +386,11 @@
         def _():
             relay(f)
 
+        @pl.when(jnp.logical_and(y == 1, f == PIECES - 1))
+        def _():
+            gm_copy(LATE - 2).wait_send()
+            gm_copy(LATE).start()
+
         @pl.when(f >= LAG)
         def _():
             finish_image(f - LAG)
@@ -404,7 +415,9 @@
 
     @pl.loop(0, PIECES)
     def _(f):
-        gm_copy(f).wait_send()
+        @pl.when(jnp.where(y == 0, f >= n_handed, jnp.logical_or(y > 1, f != LATE - 2)))
+        def _():
+            gm_copy(f).wait_send()
 
         @pl.when(jnp.logical_and(y > 0, jnp.logical_or(y != 2, f < LATE)))
         def _():

time: 70.6 us -> 70.3 us (level)
  no operation moved by 1% of the time
where the time goes in v5:
time: 70.3 us; the launch traced here: 70.1 us
  Pallas kernels  68.2 us (97%)
  between operations  1.93 us (3%)
    pallas_call x1, Pallas kernels, shards(): pl.pallas_call(functools.partial(kernel, total, fold_size), out_shape=(ja...  66 us
    pallas_call x1, Pallas kernels, shards(): pl.pallas_call(store, out_shape=(jax.ShapeDtypeStruct(block, jnp.float32)...  2.22 us

profile of v5, /device:TPU:127, one launch (start us, length us, event | category | flops | bytes accessed | tf_op | source)
XLA Modules:
  0.0 70.1 jit_solution(15527450773325434575)
XLA Ops:
  1.9 66.0 %shard_map.59 = (f32[512,1152]{1,0:T(8,128)S(1)}, f32[512,1152]{1,0:T(8,128)S(1)}) custom-call(bf16[512,1152]{1,0:T(8,128)(2,1)} %image_ref.1, bf16[512,1152]{1,0:T(8,128)(2,1)} %text_ref.1, f32[1,1]{1,0:T(1,128)} %bitcast.2.mult_ref, f32[1,1]{1,0:T(1,128)} %bitcast.3.shift_ref), custom_call_target="tpu_custom_call" | custom-call | flops 7247757312 | bytes 7077888 | tf_op jit(solution)/shard_map/pallas_call | solution.py:451
  67.9 2.2 %shard_map.60 = (f32[512,1152]{1,0:T(8,128)}, f32[512,1152]{1,0:T(8,128)}) custom-call(f32[512,1152]{1,0:T(8,128)S(1)} %get-tuple-element.4.image_ref, f32[512,1152]{1,0:T(8,128)S(1)} %get-tuple-element.5.text_ref), custom_call_target="tpu_custom_call" | custom-call | tf_op jit(solution)/shard_map/pallas_call | solution.py:486
